TPU v7x, 128 devices: a whole 4x4x4 slice. The times are simulated.
128 devices in a mesh: rows: 32 (over z, y, core), cols: 4 (over x).
Axes of the slice: x: 4, y: 4, z: 4, core: 2. Of those that a mesh axis runs over, the one named last changes fastest.
Arguments:
- basis: float32 [64, 262144], P('cols', 'rows'), may hold values from -450 to 450
- blocks: bfloat16 [1024, 4, 256, 256], P('rows'), may hold values from -16 to 1, as said below
- far_cols: int32 [1024], P('rows'), may hold values from 0 to 1023, as said below
Outputs:
- basis_out: float32 [64, 262144], P('cols', 'rows')
- ritz: float32 [64, 64], P(None, 'cols')
Inputs may be any that keep to these rules, and one draw needn't show every extreme that they name: Off-diagonal entries are positive; each diagonal entry of a diagonal block is minus the sum of the other entries of its row over the four blocks, rounded to bfloat16. `far_cols`: the block rows of one device name at most 2 far columns among the block rows of any one device; the block rows of some device are named by exactly 2 block rows of every device.
All inputs are finite; a program needn't handle non-finite values.
Results may differ from a plain program's by a relative error of at most 0.0036.
Values may be sent and summed in bfloat16 or wider, within the bound.
No kernel may reach another device: no remote copies, remote signals or barrier semaphores. Data moves between devices by JAX's collectives and lax.ppermute only.
A program may use at most 128 MiB of HBM per device.

v0:
```python
import jax
import jax.numpy as jnp
from jax import lax
from jax.sharding import PartitionSpec as P

ITERS = 4


def with_halo(block, sides, width):
    for axis, dim in sides:
        count = lax.axis_size(axis)
        forward = [(i, i + 1) for i in range(count - 1)]
        forward.append((count - 1, 0))
        backward = [(target, source) for source, target in forward]
        low = lax.ppermute(
            lax.slice_in_dim(block, block.shape[dim] - width, None, axis=dim), axis, forward
        )
        high = lax.ppermute(lax.slice_in_dim(block, 0, width, axis=dim), axis, backward)
        block = jnp.concatenate([low, block, high], axis=dim)
    return block


def block_product(pieces, blocks, position):
    return jnp.einsum(
        "jbt,bst->jbs", pieces, blocks[:, position], preferred_element_type=jnp.float32
    )


def body(basis, blocks, far_cols):
    width = basis.shape[0]
    block_rows = blocks.shape[0]
    block_size = blocks.shape[2]
    row_devices = lax.axis_size("rows")
    total_states = block_rows * block_size * row_devices
    modes = width * lax.axis_size("cols")
    highest = lax.Precision.HIGHEST

    def apply_generator(iterate_bf):
        shaped = iterate_bf.reshape(width, block_rows, block_size)
        result = block_product(shaped, blocks, 0)
        empty = jnp.zeros((width, block_rows, block_size), jnp.bfloat16)
        piece = lax.all_gather(shaped, "rows", axis=1, tiled=True)
        inside = jnp.logical_and(far_cols >= 0, far_cols < piece.shape[1])
        taken = jnp.take(piece, jnp.clip(far_cols, 0, piece.shape[1] - 1), axis=1)
        remote = jnp.where(inside[None, :, None], taken, empty)
        extended = with_halo(shaped, (("rows", 1),), 1)
        result = result + block_product(extended[:, :-2], blocks, 1)
        result = result + block_product(extended[:, 2:], blocks, 2)
        result = result + block_product(remote, blocks, 3)
        return result.reshape(width, block_rows * block_size)

    iterate = basis
    for step in range(ITERS):
        iterate = iterate + 0.2 * apply_generator(iterate.astype(jnp.bfloat16))
    whole_iterate = lax.all_gather(iterate, "cols", axis=0, tiled=True)
    contract = (((1,), (1,)), ((), ()))
    gram_part = lax.dot_general(whole_iterate, iterate, contract, precision=highest)
    column_start = lax.axis_index("cols") * width
    gram_mine = lax.psum(gram_part, "rows")
    gram = lax.all_gather(gram_mine, "cols", axis=1, tiled=True) / total_states
    applied = apply_generator(iterate.astype(jnp.bfloat16))
    product_part = lax.dot_general(whole_iterate, applied, contract, precision=highest)
    product_mine = lax.psum(product_part, "rows")
    product = lax.all_gather(product_mine, "cols", axis=1, tiled=True) / total_states
    factor = jnp.linalg.cholesky(gram)
    identity_square = jnp.eye(modes, dtype=factor.dtype)
    inverse_factor = lax.linalg.triangular_solve(
        factor, identity_square, left_side=True, lower=True
    )
    own_rows = lax.dynamic_slice_in_dim(inverse_factor, column_start, width, 0)
    basis_out = jnp.dot(own_rows, whole_iterate, precision=highest)
    left_part = jnp.dot(inverse_factor, product, precision=highest)
    ritz_whole = jnp.dot(left_part, inverse_factor.T, precision=highest)
    ritz = lax.dynamic_slice_in_dim(ritz_whole, column_start, width, 1)
    return (basis_out, ritz)


def solution(mesh):
    in_specs = (P("cols", "rows"), P("rows", None, None, None), P("rows"))
    out_specs = (P("cols", "rows"), P(None, "cols"))
    return jax.shard_map(body, mesh=mesh, in_specs=in_specs, out_specs=out_specs, check_vma=False)
```

profile of v0, /device:TPU:0, one launch (start us, length us, event | category | flops | bytes accessed | tf_op | source)
XLA Modules:
  0.0 539.1 jit_solution(13265493274930220181)
XLA Ops:
  7.2 1.1 convert_element_type.16
  8.3 0.7 copy.158
  9.1 0.7 fusion.238
  9.8 6.0 %collective-permute-start.1 = (bf16[16,1,256]{2,0,1:T(8,128)(2,1)S(1)}, bf16[16,1,256]{2,0,1:T(8,128)(2,1)S(1)}, u32[]{:S(2)}, u32[]{:S(2)}) collective-permute-start(bf16[16,1,256]{2,0,1:T(8,128)(2,1)S(1)} %get-tuple-element.23), channel_id=1, source_target_pairs={{4,0},{8,4},{12,8},{16,12},{20,16},{24,20},{28,24},{32,28},{36,32}... | collective-permute-start | bytes 24584 | tf_op jit(solution)/shard_map/ppermute | solution.py:18
  15.8 0.7 compare_and_fusion
  16.5 3.4 fusion.60
  19.9 3.6 fusion.84
  23.5 3.5 fusion.81
  27.0 39.3 %all-gather.7.cloned.1.call-done = bf16[16,1024,256]{2,0,1:T(8,128)(2,1)} async-done(((bf16[16,32,256]{2,0,1:T(8,128)(2,1)}), bf16[16,1024,256]{2,0,1:T(8,128)(2,1)}) %all-gather.7.cloned.1.call-update) | async-done | bytes 8388624 | tf_op jit(solution)/shard_map/all_gather | solution.py:42
  66.4 3.9 gather_fusion
  70.3 3.4 fusion.72
  73.9 0.7 copy.157
  74.7 0.7 fusion.237
  75.4 2.8 collective-permute-start.3
  78.2 3.4 fusion.36
  81.6 3.6 fusion.16
  85.2 42.1 %all-gather.9.cloned.1.call-done = bf16[16,1024,256]{2,0,1:T(8,128)(2,1)} async-done(((bf16[16,32,256]{2,0,1:T(8,128)(2,1)}), bf16[16,1024,256]{2,0,1:T(8,128)(2,1)}) %all-gather.9.cloned.1.call-update) | async-done | bytes 8388624 | tf_op jit(solution)/shard_map/all_gather | solution.py:42
  127.3 3.9 gather_fusion.1
  131.2 3.4 fusion.6
  134.7 3.4 fusion.141
  138.2 0.7 copy.156
  139.0 0.7 fusion.236
  139.7 2.8 collective-permute-start.5
  142.5 3.4 fusion.34
  145.9 3.6 fusion.14
  149.6 42.1 %all-gather.11.cloned.1.call-done = bf16[16,1024,256]{2,0,1:T(8,128)(2,1)} async-done(((bf16[16,32,256]{2,0,1:T(8,128)(2,1)}), bf16[16,1024,256]{2,0,1:T(8,128)(2,1)}) %all-gather.11.cloned.1.call-update) | async-done | bytes 8388624 | tf_op jit(solution)/shard_map/all_gather | solution.py:42
  191.6 3.9 gather_fusion.2
  195.6 3.4 fusion.4
  199.0 3.4 fusion.129
  202.5 0.7 copy.155
  203.3 0.7 fusion.235
  204.0 2.8 collective-permute-start.7
  206.9 3.4 fusion.32
  210.3 3.6 fusion.12
  213.9 42.1 %all-gather.13.cloned.1.call-done = bf16[16,1024,256]{2,0,1:T(8,128)(2,1)} async-done(((bf16[16,32,256]{2,0,1:T(8,128)(2,1)}), bf16[16,1024,256]{2,0,1:T(8,128)(2,1)}) %all-gather.13.cloned.1.call-update) | async-done | bytes 8388624 | tf_op jit(solution)/shard_map/all_gather | solution.py:42
  256.0 3.9 gather_fusion.3
  259.9 3.4 fusion.2
  263.3 3.4 fusion.117
  266.8 0.9 fusion.230
  267.7 0.7 copy.154
  268.5 0.7 fusion.234
  269.2 2.8 collective-permute-start.9
  272.0 3.4 fusion.30
  275.5 3.8 fusion.10
  279.3 18.8 %all-gather.15.cloned.1.call-done = f32[64,8192]{1,0:T(8,128)} async-done(((f32[16,8192]{1,0:T(8,128)}), f32[64,8192]{1,0:T(8,128)}) %all-gather.15.cloned.1.call-update) | async-done | bytes 2097168 | tf_op jit(solution)/shard_map/all_gather | solution.py:55
  298.1 3.3 fusion.239
  301.5 51.9 %all-gather.17.cloned.1.call-done = bf16[16,1024,256]{2,0,1:T(8,128)(2,1)} async-done(((bf16[16,32,256]{2,0,1:T(8,128)(2,1)}), bf16[16,1024,256]{2,0,1:T(8,128)(2,1)}) %all-gather.17.cloned.1.call-update) | async-done | bytes 8388624 | tf_op jit(solution)/shard_map/all_gather | solution.py:42
  353.3 3.9 gather_fusion.4
  357.3 3.4 fusion
  360.7 3.6 fusion.105
  364.4 1.7 fusion.240
  366.1 126.6 %all-reduce = (f32[64,16]{0,1:T(8,128)S(1)}, f32[64,16]{0,1:T(8,128)S(1)}) all-reduce(f32[64,16]{0,1:T(8,128)S(1)} %fusion.239, f32[64,16]{0,1:T(8,128)S(1)} %fusion.240), channel_id=1, replica_groups=mesh['rows'=32,'cols'=4] {'rows'}, use_global_device_ids=true, to_apply=%region_0.2 | all-reduce | flops 2048 | bytes 16384 | tf_op jit(solution)/shard_map/psum | solution.py:59
  492.6 12.4 %all_gather.29 = f32[64,64]{0,1:T(8,128)S(1)} all-gather(f32[64,16]{0,1:T(8,128)S(1)} %get-tuple-element.3), channel_id=1, replica_groups=mesh['rows'=32,'cols'=4] {'cols'}, dimensions={1}, use_global_device_ids=true | all-gather | bytes 20480 | tf_op jit(solution)/shard_map/all_gather | solution.py:60
  505.1 0.1 copy.122
  505.2 5.8 %cholesky.17 = f32[64,64]{1,0:T(8,128)S(1)} custom-call(f32[64,64]{1,0:T(8,128)S(1)} %fusion.202), custom_call_target="Cholesky" | custom-call | tf_op jit(solution)/shard_map/jit(cholesky)/cholesky | solution.py:65
  511.1 0.6 compare_reduce_fusion
  511.7 0.7 fusion.199
  512.4 4.9 custom-call.6
  517.3 0.2 fusion.200
  517.5 11.9 %all_gather.31 = f32[64,64]{0,1:T(8,128)S(1)} all-gather(f32[64,16]{0,1:T(8,128)S(1)} %get-tuple-element.4), channel_id=1, replica_groups=mesh['rows'=32,'cols'=4] {'cols'}, dimensions={1}, use_global_device_ids=true | all-gather | bytes 20480 | tf_op jit(solution)/shard_map/all_gather | solution.py:64
  529.4 0.2 fusion.203
  529.6 0.2 fusion.241
  529.8 0.6 constant_dynamic-slice_fusion
  530.4 1.9 fusion.206
  (55 shorter events, 1.0 us)
Async XLA Ops:
  7.2 59.2 %all-gather.7.cloned.1.call-start = ((), (), s32[]{:S(2)}) async-start(), calls=%async_computation | async-start | bytes 8650752 | tf_op jit(solution)/shard_map/all_gather | solution.py:42
  9.0 118.3 %all-gather.9.cloned.1.call-start = ((), (), s32[]{:S(2)}) async-start(), calls=%async_computation.1 | async-start | bytes 8650752 | tf_op jit(solution)/shard_map/all_gather | solution.py:42
  9.8 10.1 %collective-permute-start = (bf16[16,1,256]{2,0,1:T(8,128)(2,1)S(1)}, bf16[16,1,256]{2,0,1:T(8,128)(2,1)S(1)}, u32[]{:S(2)}, u32[]{:S(2)}) collective-permute-start(bf16[16,1,256]{2,0,1:T(8,128)(2,1)S(1)} %get-tuple-element.24), channel_id=1, source_target_pairs={{0,4},{4,8},{8,12},{12,16},{16,20},{20,24},{24,28},{28,32},{32,36}... | collective-permute-start | bytes 24584 | tf_op jit(solution)/shard_map/ppermute | solution.py:15
  9.8 13.7 %collective-permute-start.1 = (bf16[16,1,256]{2,0,1:T(8,128)(2,1)S(1)}, bf16[16,1,256]{2,0,1:T(8,128)(2,1)S(1)}, u32[]{:S(2)}, u32[]{:S(2)}) collective-permute-start(bf16[16,1,256]{2,0,1:T(8,128)(2,1)S(1)} %get-tuple-element.23), channel_id=1, source_target_pairs={{4,0},{8,4},{12,8},{16,12},{20,16},{24,20},{28,24},{32,28},{36,32}... | collective-permute-start | bytes 24584 | tf_op jit(solution)/shard_map/ppermute | solution.py:18
  19.9 3.6 copy-start.4
  23.5 50.3 %copy-start.2 = (f32[16,8192]{1,0:T(8,128)S(1)}, f32[16,8192]{1,0:T(8,128)}, u32[]{:S(2)}) copy-start(f32[16,8192]{1,0:T(8,128)} %param.5) | copy-start | bytes 1572868
  74.6 117.0 %all-gather.11.cloned.1.call-start = ((), (), s32[]{:S(2)}) async-start(), calls=%async_computation.2 | async-start | bytes 8650752 | tf_op jit(solution)/shard_map/all_gather | solution.py:42
  75.4 6.2 %collective-permute-start.3 = (bf16[16,1,256]{2,0,1:T(8,128)(2,1)S(1)}, bf16[16,1,256]{2,0,1:T(8,128)(2,1)S(1)}, u32[]{:S(2)}, u32[]{:S(2)}) collective-permute-start(bf16[16,1,256]{2,0,1:T(8,128)(2,1)S(1)} %get-tuple-element.22), channel_id=1, source_target_pairs={{4,0},{8,4},{12,8},{16,12},{20,16},{24,20},{28,24},{32,28},{36,32}... | collective-permute-start | bytes 24584 | tf_op jit(solution)/shard_map/ppermute | solution.py:18
  81.6 53.1 %copy-start.5 = (bf16[2,32,8,256]{3,2,0,1:T(8,128)(2,1)S(1)}, bf16[2,32,8,256]{3,2,0,1:T(8,128)(2,1)}, u32[]{:S(2)}) copy-start(bf16[2,32,8,256]{3,2,0,1:T(8,128)(2,1)} %copy.157) | copy-start | bytes 786436
  81.6 53.1 %collective-permute-start.2 = (bf16[16,1,256]{2,0,1:T(8,128)(2,1)S(1)}, bf16[16,1,256]{2,0,1:T(8,128)(2,1)S(1)}, u32[]{:S(2)}, u32[]{:S(2)}) collective-permute-start(bf16[16,1,256]{2,0,1:T(8,128)(2,1)S(1)} %get-tuple-element.21), channel_id=1, source_target_pairs={{0,4},{4,8},{8,12},{12,16},{16,20},{20,24},{24,28},{28,32},{32,36}... | collective-permute-start | bytes 24584 | tf_op jit(solution)/shard_map/ppermute | solution.py:15
  138.9 117.0 %all-gather.13.cloned.1.call-start = ((), (), s32[]{:S(2)}) async-start(), calls=%async_computation.3 | async-start | bytes 8650752 | tf_op jit(solution)/shard_map/all_gather | solution.py:42
  139.7 6.2 %collective-permute-start.5 = (bf16[16,1,256]{2,0,1:T(8,128)(2,1)S(1)}, bf16[16,1,256]{2,0,1:T(8,128)(2,1)S(1)}, u32[]{:S(2)}, u32[]{:S(2)}) collective-permute-start(bf16[16,1,256]{2,0,1:T(8,128)(2,1)S(1)} %get-tuple-element.20), channel_id=1, source_target_pairs={{4,0},{8,4},{12,8},{16,12},{20,16},{24,20},{28,24},{32,28},{36,32}... | collective-permute-start | bytes 24584 | tf_op jit(solution)/shard_map/ppermute | solution.py:18
  145.9 53.1 %copy-start.6 = (bf16[2,32,8,256]{3,2,0,1:T(8,128)(2,1)S(1)}, bf16[2,32,8,256]{3,2,0,1:T(8,128)(2,1)}, u32[]{:S(2)}) copy-start(bf16[2,32,8,256]{3,2,0,1:T(8,128)(2,1)} %copy.156) | copy-start | bytes 786436
  145.9 53.1 %collective-permute-start.4 = (bf16[16,1,256]{2,0,1:T(8,128)(2,1)S(1)}, bf16[16,1,256]{2,0,1:T(8,128)(2,1)S(1)}, u32[]{:S(2)}, u32[]{:S(2)}) collective-permute-start(bf16[16,1,256]{2,0,1:T(8,128)(2,1)S(1)} %get-tuple-element.19), channel_id=1, source_target_pairs={{0,4},{4,8},{8,12},{12,16},{16,20},{20,24},{24,28},{28,32},{32,36}... | collective-permute-start | bytes 24584 | tf_op jit(solution)/shard_map/ppermute | solution.py:15
  203.3 94.9 %all-gather.15.cloned.1.call-start = ((), (), s32[]{:S(2)}) async-start(), calls=%async_computation.4 | async-start | bytes 2621440 | tf_op jit(solution)/shard_map/all_gather | solution.py:55
  204.0 6.2 %collective-permute-start.7 = (bf16[16,1,256]{2,0,1:T(8,128)(2,1)S(1)}, bf16[16,1,256]{2,0,1:T(8,128)(2,1)S(1)}, u32[]{:S(2)}, u32[]{:S(2)}) collective-permute-start(bf16[16,1,256]{2,0,1:T(8,128)(2,1)S(1)} %get-tuple-element.18), channel_id=1, source_target_pairs={{4,0},{8,4},{12,8},{16,12},{20,16},{24,20},{28,24},{32,28},{36,32}... | collective-permute-start | bytes 24584 | tf_op jit(solution)/shard_map/ppermute | solution.py:18
  210.3 53.1 %copy-start.7 = (bf16[2,32,8,256]{3,2,0,1:T(8,128)(2,1)S(1)}, bf16[2,32,8,256]{3,2,0,1:T(8,128)(2,1)}, u32[]{:S(2)}) copy-start(bf16[2,32,8,256]{3,2,0,1:T(8,128)(2,1)} %copy.155) | copy-start | bytes 786436
  210.3 53.1 %collective-permute-start.6 = (bf16[16,1,256]{2,0,1:T(8,128)(2,1)S(1)}, bf16[16,1,256]{2,0,1:T(8,128)(2,1)S(1)}, u32[]{:S(2)}, u32[]{:S(2)}) collective-permute-start(bf16[16,1,256]{2,0,1:T(8,128)(2,1)S(1)} %get-tuple-element.17), channel_id=1, source_target_pairs={{0,4},{4,8},{8,12},{12,16},{16,20},{20,24},{24,28},{28,32},{32,36}... | collective-permute-start | bytes 24584 | tf_op jit(solution)/shard_map/ppermute | solution.py:15
  267.7 85.7 %all-gather.17.cloned.1.call-start = ((), (), s32[]{:S(2)}) async-start(), calls=%async_computation.5 | async-start | bytes 8650752 | tf_op jit(solution)/shard_map/all_gather | solution.py:42
  269.2 6.2 %collective-permute-start.9 = (bf16[16,1,256]{2,0,1:T(8,128)(2,1)S(1)}, bf16[16,1,256]{2,0,1:T(8,128)(2,1)S(1)}, u32[]{:S(2)}, u32[]{:S(2)}) collective-permute-start(bf16[16,1,256]{2,0,1:T(8,128)(2,1)S(1)} %get-tuple-element.16), channel_id=1, source_target_pairs={{4,0},{8,4},{12,8},{16,12},{20,16},{24,20},{28,24},{32,28},{36,32}... | collective-permute-start | bytes 24584 | tf_op jit(solution)/shard_map/ppermute | solution.py:18
  275.4 22.7 %copy-start.1 = (f32[16,8192]{1,0:T(8,128)S(1)}, f32[16,8192]{1,0:T(8,128)}, u32[]{:S(2)}) copy-start(f32[16,8192]{1,0:T(8,128)} %get-tuple-element.6) | copy-start | bytes 1572868
  275.4 85.3 %copy-start.3 = (bf16[2,32,8,256]{3,2,0,1:T(8,128)(2,1)S(1)}, bf16[2,32,8,256]{3,2,0,1:T(8,128)(2,1)}, u32[]{:S(2)}) copy-start(bf16[2,32,8,256]{3,2,0,1:T(8,128)(2,1)} %copy.154) | copy-start | bytes 786436
  275.4 85.3 %collective-permute-start.8 = (bf16[16,1,256]{2,0,1:T(8,128)(2,1)S(1)}, bf16[16,1,256]{2,0,1:T(8,128)(2,1)S(1)}, u32[]{:S(2)}, u32[]{:S(2)}) collective-permute-start(bf16[16,1,256]{2,0,1:T(8,128)(2,1)S(1)} %get-tuple-element.15), channel_id=1, source_target_pairs={{0,4},{4,8},{8,12},{12,16},{16,20},{20,24},{24,28},{28,32},{32,36}... | collective-permute-start | bytes 24584 | tf_op jit(solution)/shard_map/ppermute | solution.py:15
  360.7 3.6 copy-start
Sparse Core Ops, SparseCore 0:
  10.8 55.4 all-gather.6
  74.7 52.5 all-gather.8
  139.1 52.5 all-gather.10
  203.4 52.5 all-gather.12
  267.8 30.2 all-gather.14
  300.2 53.0 all-gather.16
where the time goes:
time: 540 us; the launch traced here: 539 us
  waiting for transfers between devices  236 us (44%)
  blocking collectives  151 us (28%)
  matrix products  77.1 us (14%)
  local copies, waits for them, and re-layouts  27.9 us (5%)
  starting transfers between devices  17.6 us (3%)
  other arithmetic  14.9 us (3%)
  between operations  14.4 us (3%)
    all_gather x5, waiting for transfers between devices, apply_generator(): piece = lax.all_gather(shaped, 'rows', axis=1, tiled=True)  217 us
    psum x1, blocking collectives, body(): gram_mine = lax.psum(gram_part, 'rows')  127 us
    dot_general x20, matrix products, block_product(): jnp.einsum('jbt,bst->jbs', pieces, blocks[:, position], preferred_element...  69.5 us
    gather x5, local copies, waits for them, and re-layouts, apply_generator(): taken = jnp.take(piece, jnp.clip(far_cols, 0, piece.shape[1] - 1), axis=1)  19.7 us
    all_gather x1, waiting for transfers between devices, body(): whole_iterate = lax.all_gather(iterate, 'cols', axis=0, tiled=True)  18.8 us
    ppermute x5, starting transfers between devices, with_halo(): lax.ppermute(lax.slice_in_dim(block, 0, width, axis=dim), axis, backward)  17.3 us
    all_gather x1, blocking collectives, body(): gram = lax.all_gather(gram_mine, 'cols', axis=1, tiled=True) / total_states  12.4 us
    all_gather x1, blocking collectives, body(): lax.all_gather(product_mine, 'cols', axis=1, tiled=True) / total_states  11.9 us
  transfers between devices with their start and end apart: 16, of which 6 were waited for; matrix products, arithmetic and copies ran while one was open for 14% of the time, Pallas kernels for 0%

commit v1 on v0

--- a/solution.py
+++ b/solution.py
@@ -56,7 +56,7 @@
     contract = (((1,), (1,)), ((), ()))
     gram_part = lax.dot_general(whole_iterate, iterate, contract, precision=highest)
     column_start = lax.axis_index("cols") * width
-    gram_mine = lax.psum(gram_part, "rows")
+    gram_mine = jnp.sum(jax.lax.all_gather(gram_part, axis_name="rows"), 0)
     gram = lax.all_gather(gram_mine, "cols", axis=1, tiled=True) / total_states
     applied = apply_generator(iterate.astype(jnp.bfloat16))
     product_part = lax.dot_general(whole_iterate, applied, contract, precision=highest)

time: 540 us -> 454 us (0.84)
  waiting for transfers between devices: 236 us -> 184 us
  blocking collectives: 151 us -> 115 us
    psum x1, blocking collectives: 127 us -> 65.3 us  [body(): product_mine = lax.psum(product_part, 'rows')]
    all_gather x5, waiting for transfers between devices: 217 us -> 166 us  [apply_generator(): piece = lax.all_gather(shaped, 'rows', axis=1, tiled=True)]
    all_gather x0 -> x1, blocking collectives: none -> 25 us  [body(): gram_mine = jnp.sum(jax.lax.all_gather(gram_part, axis_name='rows'), 0)]
  transfers between devices with their start and end apart: 16 -> 16, of which waited for: 6 -> 5; matrix products, arithmetic and copies ran while one was open for 14% -> 20% of each run, Pallas kernels for 0% -> 0%
where the time goes in v1:
time: 454 us; the launch traced here: 453 us
  waiting for transfers between devices  184 us (41%)
  blocking collectives  115 us (25%)
  matrix products  78.7 us (17%)
  local copies, waits for them, and re-layouts  27.9 us (6%)
  starting transfers between devices  17.5 us (4%)
  other arithmetic  14.9 us (3%)
  between operations  14.5 us (3%)
    all_gather x5, waiting for transfers between devices, apply_generator(): piece = lax.all_gather(shaped, 'rows', axis=1, tiled=True)  166 us
    dot_general x20, matrix products, block_product(): jnp.einsum('jbt,bst->jbs', pieces, blocks[:, position], preferred_element...  69.5 us
    psum x1, blocking collectives, body(): product_mine = lax.psum(product_part, 'rows')  65.3 us
    all_gather x1, blocking collectives, body(): gram_mine = jnp.sum(jax.lax.all_gather(gram_part, axis_name='rows'), 0)  25 us
    gather x5, local copies, waits for them, and re-layouts, apply_generator(): taken = jnp.take(piece, jnp.clip(far_cols, 0, piece.shape[1] - 1), axis=1)  19.7 us
    all_gather x1, waiting for transfers between devices, body(): whole_iterate = lax.all_gather(iterate, 'cols', axis=0, tiled=True)  18.9 us
    ppermute x5, starting transfers between devices, with_halo(): lax.ppermute(lax.slice_in_dim(block, 0, width, axis=dim), axis, backward)  17.3 us
    all_gather x1, blocking collectives, body(): lax.all_gather(product_mine, 'cols', axis=1, tiled=True) / total_states  12.2 us
  transfers between devices with their start and end apart: 16, of which 5 were waited for; matrix products, arithmetic and copies ran while one was open for 20% of the time, Pallas kernels for 0%

profile of v1, /device:TPU:0, one launch (start us, length us, event | category | flops | bytes accessed | tf_op | source)
XLA Modules:
  0.0 452.6 jit_solution(6914848809600684148)
XLA Ops:
  7.2 1.1 convert_element_type.16
  8.3 0.7 copy.158
  9.1 0.7 fusion.238
  9.8 6.0 %collective-permute-start.1 = (bf16[16,1,256]{2,0,1:T(8,128)(2,1)S(1)}, bf16[16,1,256]{2,0,1:T(8,128)(2,1)S(1)}, u32[]{:S(2)}, u32[]{:S(2)}) collective-permute-start(bf16[16,1,256]{2,0,1:T(8,128)(2,1)S(1)} %get-tuple-element.21), channel_id=1, source_target_pairs={{4,0},{8,4},{12,8},{16,12},{20,16},{24,20},{28,24},{32,28},{36,32}... | collective-permute-start | bytes 24584 | tf_op jit(solution)/shard_map/ppermute | solution.py:18
  15.8 0.7 compare_and_fusion
  16.5 3.4 fusion.60
  19.9 3.6 fusion.84
  23.5 3.5 fusion.81
  27.0 39.3 %all-gather.9.cloned.1.call-done = bf16[16,1024,256]{2,0,1:T(8,128)(2,1)} async-done(((bf16[16,32,256]{2,0,1:T(8,128)(2,1)}), bf16[16,1024,256]{2,0,1:T(8,128)(2,1)}) %all-gather.9.cloned.1.call-update) | async-done | bytes 8388624 | tf_op jit(solution)/shard_map/all_gather | solution.py:42
  66.4 3.9 gather_fusion
  70.3 3.4 fusion.72
  73.9 0.7 copy.157
  74.7 0.7 fusion.237
  75.4 2.8 collective-permute-start.3
  78.2 3.4 fusion.36
  81.6 3.6 fusion.16
  85.2 42.1 %all-gather.11.cloned.1.call-done = bf16[16,1024,256]{2,0,1:T(8,128)(2,1)} async-done(((bf16[16,32,256]{2,0,1:T(8,128)(2,1)}), bf16[16,1024,256]{2,0,1:T(8,128)(2,1)}) %all-gather.11.cloned.1.call-update) | async-done | bytes 8388624 | tf_op jit(solution)/shard_map/all_gather | solution.py:42
  127.3 3.9 gather_fusion.1
  131.2 3.4 fusion.6
  134.7 3.4 fusion.141
  138.2 0.7 copy.156
  139.0 0.7 fusion.236
  139.7 2.8 collective-permute-start.5
  142.5 3.4 fusion.34
  145.9 3.6 fusion.14
  149.6 42.1 %all-gather.13.cloned.1.call-done = bf16[16,1024,256]{2,0,1:T(8,128)(2,1)} async-done(((bf16[16,32,256]{2,0,1:T(8,128)(2,1)}), bf16[16,1024,256]{2,0,1:T(8,128)(2,1)}) %all-gather.13.cloned.1.call-update) | async-done | bytes 8388624 | tf_op jit(solution)/shard_map/all_gather | solution.py:42
  191.6 3.9 gather_fusion.2
  195.6 3.4 fusion.4
  199.0 3.4 fusion.129
  202.5 0.7 copy.155
  203.3 0.7 fusion.235
  204.0 2.8 collective-permute-start.7
  206.9 3.4 fusion.32
  210.3 3.6 fusion.12
  213.9 42.1 %all-gather.15.cloned.1.call-done = bf16[16,1024,256]{2,0,1:T(8,128)(2,1)} async-done(((bf16[16,32,256]{2,0,1:T(8,128)(2,1)}), bf16[16,1024,256]{2,0,1:T(8,128)(2,1)}) %all-gather.15.cloned.1.call-update) | async-done | bytes 8388624 | tf_op jit(solution)/shard_map/all_gather | solution.py:42
  256.0 3.9 gather_fusion.3
  259.9 3.4 fusion.2
  263.3 3.4 fusion.117
  266.8 0.9 fusion.230
  267.7 0.7 copy.154
  268.5 0.7 fusion.234
  269.2 2.8 collective-permute-start.9
  272.0 3.4 fusion.30
  275.4 3.8 fusion.10
  279.3 18.9 %all-gather.17.cloned.1.call-done = f32[64,8192]{1,0:T(8,128)} async-done(((f32[16,8192]{1,0:T(8,128)}), f32[64,8192]{1,0:T(8,128)}) %all-gather.17.cloned.1.call-update) | async-done | bytes 2097168 | tf_op jit(solution)/shard_map/all_gather | solution.py:55
  298.1 3.3 convolution_bitcast_fusion
  301.5 25.0 %all-gather.1 = f32[32,64,16]{1,2,0:T(8,128)S(1)} all-gather(f32[1,64,16]{1,2,0:T(8,128)S(1)} %convolution_bitcast_fusion), channel_id=2, replica_groups=mesh['rows'=32,'cols'=4] {'rows'}, dimensions={0}, use_global_device_ids=true | all-gather | bytes 135168 | tf_op jit(solution)/shard_map/all_gather | solution.py:59
  326.5 12.1 %all_gather.37 = f32[64,64]{0,1:T(8,128)S(1)} all-gather(f32[64,16]{0,1:T(8,128)S(1)} %reduce_sum.9), channel_id=1, replica_groups=mesh['rows'=32,'cols'=4] {'cols'}, dimensions={1}, use_global_device_ids=true | all-gather | bytes 20480 | tf_op jit(solution)/shard_map/all_gather | solution.py:60
  338.6 0.1 copy.122
  338.7 5.8 %cholesky.17 = f32[64,64]{1,0:T(8,128)S(1)} custom-call(f32[64,64]{1,0:T(8,128)S(1)} %fusion.202), custom_call_target="Cholesky" | custom-call | tf_op jit(solution)/shard_map/jit(cholesky)/cholesky | solution.py:65
  344.6 0.6 compare_reduce_fusion
  345.3 0.7 fusion.199
  345.9 4.9 %custom-call.6 = f32[1,64,64]{1,2,0:T(8,128)S(1)} custom-call(f32[1,64,64]{2,1,0:T(8,128)S(1)} %fusion.199), custom_call_target="InvertDiagBlocksLowerTriangular" | custom-call | tf_op jit(solution)/shard_map/triangular_solve | solution.py:67
  350.8 0.2 fusion.200
  351.1 3.5 fusion.206
  354.6 3.9 gather_fusion.4
  358.5 3.4 fusion
  361.9 3.5 fusion.105
  365.5 1.7 fusion.239
  367.3 65.3 %psum.7 = f32[64,16]{0,1:T(8,128)S(1)} all-reduce(f32[64,16]{0,1:T(8,128)S(1)} %fusion.239), channel_id=1, replica_groups=mesh['rows'=32,'cols'=4] {'rows'}, use_global_device_ids=true, to_apply=%region_3.5 | all-reduce | flops 1024 | bytes 8192 | tf_op jit(solution)/shard_map/psum | solution.py:63
  432.6 12.2 %all_gather.39 = f32[64,64]{0,1:T(8,128)S(1)} all-gather(f32[64,16]{0,1:T(8,128)S(1)} %psum.7), channel_id=1, replica_groups=mesh['rows'=32,'cols'=4] {'cols'}, dimensions={1}, use_global_device_ids=true | all-gather | bytes 20480 | tf_op jit(solution)/shard_map/all_gather | solution.py:64
  444.8 0.2 fusion.203
  445.0 0.2 fusion.240
  445.2 0.6 constant_dynamic-slice_fusion
  (57 shorter events, 1.0 us)
Async XLA Ops:
  7.2 59.2 %all-gather.9.cloned.1.call-start = ((), (), s32[]{:S(2)}) async-start(), calls=%async_computation | async-start | bytes 8650752 | tf_op jit(solution)/shard_map/all_gather | solution.py:42
  9.0 118.3 %all-gather.11.cloned.1.call-start = ((), (), s32[]{:S(2)}) async-start(), calls=%async_computation.1 | async-start | bytes 8650752 | tf_op jit(solution)/shard_map/all_gather | solution.py:42
  9.8 10.1 %collective-permute-start = (bf16[16,1,256]{2,0,1:T(8,128)(2,1)S(1)}, bf16[16,1,256]{2,0,1:T(8,128)(2,1)S(1)}, u32[]{:S(2)}, u32[]{:S(2)}) collective-permute-start(bf16[16,1,256]{2,0,1:T(8,128)(2,1)S(1)} %get-tuple-element.22), channel_id=1, source_target_pairs={{0,4},{4,8},{8,12},{12,16},{16,20},{20,24},{24,28},{28,32},{32,36}... | collective-permute-start | bytes 24584 | tf_op jit(solution)/shard_map/ppermute | solution.py:15
  9.8 13.7 %collective-permute-start.1 = (bf16[16,1,256]{2,0,1:T(8,128)(2,1)S(1)}, bf16[16,1,256]{2,0,1:T(8,128)(2,1)S(1)}, u32[]{:S(2)}, u32[]{:S(2)}) collective-permute-start(bf16[16,1,256]{2,0,1:T(8,128)(2,1)S(1)} %get-tuple-element.21), channel_id=1, source_target_pairs={{4,0},{8,4},{12,8},{16,12},{20,16},{24,20},{28,24},{32,28},{36,32}... | collective-permute-start | bytes 24584 | tf_op jit(solution)/shard_map/ppermute | solution.py:18
  19.9 3.6 copy-start.4
  23.5 50.3 %copy-start.2 = (f32[16,8192]{1,0:T(8,128)S(1)}, f32[16,8192]{1,0:T(8,128)}, u32[]{:S(2)}) copy-start(f32[16,8192]{1,0:T(8,128)} %param.5) | copy-start | bytes 1572868
  74.6 117.0 %all-gather.13.cloned.1.call-start = ((), (), s32[]{:S(2)}) async-start(), calls=%async_computation.2 | async-start | bytes 8650752 | tf_op jit(solution)/shard_map/all_gather | solution.py:42
  75.4 6.2 %collective-permute-start.3 = (bf16[16,1,256]{2,0,1:T(8,128)(2,1)S(1)}, bf16[16,1,256]{2,0,1:T(8,128)(2,1)S(1)}, u32[]{:S(2)}, u32[]{:S(2)}) collective-permute-start(bf16[16,1,256]{2,0,1:T(8,128)(2,1)S(1)} %get-tuple-element.20), channel_id=1, source_target_pairs={{4,0},{8,4},{12,8},{16,12},{20,16},{24,20},{28,24},{32,28},{36,32}... | collective-permute-start | bytes 24584 | tf_op jit(solution)/shard_map/ppermute | solution.py:18
  81.6 53.1 %copy-start.5 = (bf16[2,32,8,256]{3,2,0,1:T(8,128)(2,1)S(1)}, bf16[2,32,8,256]{3,2,0,1:T(8,128)(2,1)}, u32[]{:S(2)}) copy-start(bf16[2,32,8,256]{3,2,0,1:T(8,128)(2,1)} %copy.157) | copy-start | bytes 786436
  81.6 53.1 %collective-permute-start.2 = (bf16[16,1,256]{2,0,1:T(8,128)(2,1)S(1)}, bf16[16,1,256]{2,0,1:T(8,128)(2,1)S(1)}, u32[]{:S(2)}, u32[]{:S(2)}) collective-permute-start(bf16[16,1,256]{2,0,1:T(8,128)(2,1)S(1)} %get-tuple-element.19), channel_id=1, source_target_pairs={{0,4},{4,8},{8,12},{12,16},{16,20},{20,24},{24,28},{28,32},{32,36}... | collective-permute-start | bytes 24584 | tf_op jit(solution)/shard_map/ppermute | solution.py:15
  138.9 117.0 %all-gather.15.cloned.1.call-start = ((), (), s32[]{:S(2)}) async-start(), calls=%async_computation.3 | async-start | bytes 8650752 | tf_op jit(solution)/shard_map/all_gather | solution.py:42
  139.7 6.2 %collective-permute-start.5 = (bf16[16,1,256]{2,0,1:T(8,128)(2,1)S(1)}, bf16[16,1,256]{2,0,1:T(8,128)(2,1)S(1)}, u32[]{:S(2)}, u32[]{:S(2)}) collective-permute-start(bf16[16,1,256]{2,0,1:T(8,128)(2,1)S(1)} %get-tuple-element.18), channel_id=1, source_target_pairs={{4,0},{8,4},{12,8},{16,12},{20,16},{24,20},{28,24},{32,28},{36,32}... | collective-permute-start | bytes 24584 | tf_op jit(solution)/shard_map/ppermute | solution.py:18
  145.9 53.1 %copy-start.6 = (bf16[2,32,8,256]{3,2,0,1:T(8,128)(2,1)S(1)}, bf16[2,32,8,256]{3,2,0,1:T(8,128)(2,1)}, u32[]{:S(2)}) copy-start(bf16[2,32,8,256]{3,2,0,1:T(8,128)(2,1)} %copy.156) | copy-start | bytes 786436
  145.9 53.1 %collective-permute-start.4 = (bf16[16,1,256]{2,0,1:T(8,128)(2,1)S(1)}, bf16[16,1,256]{2,0,1:T(8,128)(2,1)S(1)}, u32[]{:S(2)}, u32[]{:S(2)}) collective-permute-start(bf16[16,1,256]{2,0,1:T(8,128)(2,1)S(1)} %get-tuple-element.17), channel_id=1, source_target_pairs={{0,4},{4,8},{8,12},{12,16},{16,20},{20,24},{24,28},{28,32},{32,36}... | collective-permute-start | bytes 24584 | tf_op jit(solution)/shard_map/ppermute | solution.py:15
  203.3 94.9 %all-gather.17.cloned.1.call-start = ((), (), s32[]{:S(2)}) async-start(), calls=%async_computation.4 | async-start | bytes 2621440 | tf_op jit(solution)/shard_map/all_gather | solution.py:55
  204.0 6.2 %collective-permute-start.7 = (bf16[16,1,256]{2,0,1:T(8,128)(2,1)S(1)}, bf16[16,1,256]{2,0,1:T(8,128)(2,1)S(1)}, u32[]{:S(2)}, u32[]{:S(2)}) collective-permute-start(bf16[16,1,256]{2,0,1:T(8,128)(2,1)S(1)} %get-tuple-element.16), channel_id=1, source_target_pairs={{4,0},{8,4},{12,8},{16,12},{20,16},{24,20},{28,24},{32,28},{36,32}... | collective-permute-start | bytes 24584 | tf_op jit(solution)/shard_map/ppermute | solution.py:18
  210.3 53.1 %copy-start.7 = (bf16[2,32,8,256]{3,2,0,1:T(8,128)(2,1)S(1)}, bf16[2,32,8,256]{3,2,0,1:T(8,128)(2,1)}, u32[]{:S(2)}) copy-start(bf16[2,32,8,256]{3,2,0,1:T(8,128)(2,1)} %copy.155) | copy-start | bytes 786436
  210.3 53.1 %collective-permute-start.6 = (bf16[16,1,256]{2,0,1:T(8,128)(2,1)S(1)}, bf16[16,1,256]{2,0,1:T(8,128)(2,1)S(1)}, u32[]{:S(2)}, u32[]{:S(2)}) collective-permute-start(bf16[16,1,256]{2,0,1:T(8,128)(2,1)S(1)} %get-tuple-element.15), channel_id=1, source_target_pairs={{0,4},{4,8},{8,12},{12,16},{16,20},{20,24},{24,28},{28,32},{32,36}... | collective-permute-start | bytes 24584 | tf_op jit(solution)/shard_map/ppermute | solution.py:15
  267.7 86.9 %all-gather.19.cloned.1.call-start = ((), (), s32[]{:S(2)}) async-start(), calls=%async_computation.5 | async-start | bytes 8650752 | tf_op jit(solution)/shard_map/all_gather | solution.py:42
  269.2 6.2 %collective-permute-start.9 = (bf16[16,1,256]{2,0,1:T(8,128)(2,1)S(1)}, bf16[16,1,256]{2,0,1:T(8,128)(2,1)S(1)}, u32[]{:S(2)}, u32[]{:S(2)}) collective-permute-start(bf16[16,1,256]{2,0,1:T(8,128)(2,1)S(1)} %get-tuple-element.14), channel_id=1, source_target_pairs={{4,0},{8,4},{12,8},{16,12},{20,16},{24,20},{28,24},{32,28},{36,32}... | collective-permute-start | bytes 24584 | tf_op jit(solution)/shard_map/ppermute | solution.py:18
  275.4 22.7 %copy-start.1 = (f32[16,8192]{1,0:T(8,128)S(1)}, f32[16,8192]{1,0:T(8,128)}, u32[]{:S(2)}) copy-start(f32[16,8192]{1,0:T(8,128)} %get-tuple-element.4) | copy-start | bytes 1572868
  275.4 86.5 %collective-permute-start.8 = (bf16[16,1,256]{2,0,1:T(8,128)(2,1)S(1)}, bf16[16,1,256]{2,0,1:T(8,128)(2,1)S(1)}, u32[]{:S(2)}, u32[]{:S(2)}) collective-permute-start(bf16[16,1,256]{2,0,1:T(8,128)(2,1)S(1)} %get-tuple-element.13), channel_id=1, source_target_pairs={{0,4},{4,8},{8,12},{12,16},{16,20},{20,24},{24,28},{28,32},{32,36}... | collective-permute-start | bytes 24584 | tf_op jit(solution)/shard_map/ppermute | solution.py:15
  279.3 82.7 %copy-start.3 = (bf16[2,32,8,256]{3,2,0,1:T(8,128)(2,1)S(1)}, bf16[2,32,8,256]{3,2,0,1:T(8,128)(2,1)}, u32[]{:S(2)}) copy-start(bf16[2,32,8,256]{3,2,0,1:T(8,128)(2,1)} %copy.154) | copy-start | bytes 786436
  361.9 3.6 copy-start
Sparse Core Ops, SparseCore 0:
  10.8 55.4 all-gather.8
  74.7 52.5 all-gather.10
  139.1 52.5 all-gather.12
  203.4 52.5 all-gather.14
  267.8 30.2 all-gather.16
  300.2 53.0 all-gather.18
